TPU v7x, 32 devices: a whole 2x2x4 slice. The times are simulated.
32 devices in a mesh: ctx: 2 (over x), tp: 4 (over z), dp: 4 (over y, core).
Axes of the slice: x: 2, y: 2, z: 4, core: 2. Of those that a mesh axis runs over, the one named last changes fastest.
Arguments:
- trailing_questions: bfloat16 [1024, 8192], P(('dp', 'ctx'), 'tp'), parts along dimension 0, may hold values from -6 to 6
- output_gradient: bfloat16 [1024, 8192], P(('dp', 'ctx'), 'tp'), parts along dimension 0, may hold values from -6 to 6
- tail_row_key: bfloat16 [1024, 1024], P(('dp', 'ctx'), 'tp'), parts along dimension 0, may hold values from -6 to 6
- tail_row_value: bfloat16 [1024, 1024], P(('dp', 'ctx'), 'tp'), parts along dimension 0, may hold values from -6 to 6
- passage_key_cache: bfloat16 [2048, 1024], P(('dp', 'ctx'), 'tp'), parts along dimension 0, may hold values from -6 to 6
- passage_value_cache: bfloat16 [2048, 1024], P(('dp', 'ctx'), 'tp'), parts along dimension 0, may hold values from -6 to 6
- row_list: int32 [1024], P(('dp', 'ctx')), parts along dimension 0, may hold values from 0 to 1, as said below
- read_owner: int32 [8, 24], P(('dp', 'ctx')), parts along dimension 0, may hold values from 0 to 1, as said below
- read_tile: int32 [8, 24], P(('dp', 'ctx')), parts along dimension 0, may hold values from 0 to 1
- read_list: int32 [8, 24], P(('dp', 'ctx')), parts along dimension 0, may hold values from 0 to 1
- read_count: int32 [8], P(('dp', 'ctx')), parts along dimension 0, may hold values from 12 to 24, as said below
Outputs:
- grad_query: bfloat16 [1024, 8192], P(('dp', 'ctx'), 'tp'), parts along dimension 0
- grad_tail_key: bfloat16 [1024, 1024], P(('dp', 'ctx'), 'tp'), parts along dimension 0
- grad_tail_value: bfloat16 [1024, 1024], P(('dp', 'ctx'), 'tp'), parts along dimension 0
- grad_key_cache: float32 [2048, 1024], P(('dp', 'ctx'), 'tp'), parts along dimension 0
- grad_value_cache: float32 [2048, 1024], P(('dp', 'ctx'), 'tp'), parts along dimension 0
There are 4 independent parts, one for each index of `dp`. A program takes and returns all parts, laid end to end along the dimension named above; each array names one. Nothing has to cross between parts.
Inputs may be any that keep to these rules, and one draw needn't show every extreme that they name: `row_list`: on each reader's 128 rows the list number is 0 on a first run and 1 on the rest; both runs are nonempty. `read_owner`: a reader names one owner at most 12 times, and every reader names some owner exactly 12 times. `read_count`: some reader has all 24 reads live.
All inputs are finite; a program needn't handle non-finite values.
Results may differ from a plain program's by a relative error of at most 0.012.
Values may be sent and summed in bfloat16 or wider, within the bound.
No kernel may reach another device: no remote copies, remote signals or barrier semaphores. Data moves between devices by JAX's collectives and lax.ppermute only.
A program may use at most 64 MiB of HBM per device.

v0:
```python
import functools
import math

import jax
import jax.numpy as jnp
from jax import lax
from jax.experimental import pallas as pl
from jax.experimental.pallas import tpu as pltpu
from jax.sharding import PartitionSpec as P

WIDTH = 128
TILE = 128
PAIR = 2 * WIDTH
NEG = -1e30
SCALE = 1.0 / math.sqrt(WIDTH)
SCALE2 = SCALE * math.log2(math.e)
F32 = jnp.float32
BF16 = jnp.bfloat16


def dot_nt(a, b):
    return lax.dot_general(a, b, (((1,), (1,)), ((), ())), preferred_element_type=F32)


def dot_nn(a, b):
    return lax.dot_general(a, b, (((1,), (0,)), ((), ())), preferred_element_type=F32)


def dot_tn(a, b):
    return lax.dot_general(a, b, (((0,), (0,)), ((), ())), preferred_element_type=F32)


def repeat(steps, unroll, step):
    if unroll:
        for i in range(steps):
            step(i)
    else:

        def one(i, carry):
            step(i)
            return carry

        lax.fori_loop(0, steps, one, 0)


def columns(i, width):
    if isinstance(i, int):
        return pl.ds(i * width, width)
    return pl.ds(pl.multiple_of(i * width, width), width)


def pair_rows(ref, i):
    block = ref[:, columns(i, PAIR)]
    return jnp.concatenate([block[:, :WIDTH], block[:, WIDTH:]], axis=0)


def stacked_rows(ref, head, group):
    first = head * group
    return jnp.concatenate(
        [ref[:, (first + g) * WIDTH : (first + g + 1) * WIDTH] for g in range(group)], axis=0
    )


def twice(row):
    return jnp.concatenate([row, row], axis=1)


def tile_bias(table, first, tiles):
    return [twice(table[first + t : first + t + 1, :]) for t in range(tiles)]


def add_tiles(scores, biases):
    parts = [
        scores[t * TILE : (t + 1) * TILE, :] * SCALE2 + bias for t, bias in enumerate(biases)
    ]
    return parts[0] if len(parts) == 1 else jnp.concatenate(parts, axis=0)


def tail_bias(row_list):
    rows = row_list.shape[1]
    cut = jnp.sum((row_list == 0).astype(jnp.int32), axis=1, keepdims=True)
    key_at = lax.broadcasted_iota(jnp.int32, (rows, rows), 0)
    row_at = lax.broadcasted_iota(jnp.int32, (rows, rows), 1)
    allowed = ((key_at < cut) == (row_at < cut)) & (key_at <= row_at)
    return twice(jnp.where(allowed, 0.0, NEG).astype(F32))


def near_kernel(
    ctx, q_in, g_in, tk_in, tv_in, ok_in, ov_in, rl_in, ro_in, rt_in, rs_in, rc_ref,
    q_ref, g_ref, k_ref, p_ref, d_ref, stats_ref, table_ref,
    v_ref, rl_ref, ro_ref, rt_ref, rs_ref, sems,
):
    tail = tk_in.shape[0]
    own = ok_in.shape[0] // TILE
    heads = tk_in.shape[1] // WIDTH
    pairs = q_ref.shape[1] // PAIR
    reads = ro_ref.shape[1]
    slots = table_ref.shape[0]
    moves = [
        (rl_in, rl_ref), (ro_in, ro_ref), (rt_in, rt_ref), (rs_in, rs_ref),
        (tk_in, k_ref.at[:tail]), (ok_in, k_ref.at[tail:]), (q_in, q_ref),
        (tv_in, v_ref.at[:tail]), (ov_in, v_ref.at[tail:]), (g_in, g_ref),
    ]
    copies = [pltpu.make_async_copy(a, b, sems.at[i]) for i, (a, b) in enumerate(moves)]
    for copy in copies:
        copy.start()
    for copy in copies[:4]:
        copy.wait()
    row_list = rl_ref[...]
    owner = ro_ref[...] - lax.axis_index("ctx")
    owner = jnp.where(owner < 0, owner + ctx, owner)
    wanted = owner * own + rt_ref[...]
    live = lax.broadcasted_iota(jnp.int32, (1, reads), 1) < rc_ref[0]
    wanted = jnp.where(live, wanted, -1)
    hit = lax.broadcasted_iota(jnp.int32, (slots, reads), 0) == wanted
    first = rs_ref[...] == 0
    count0 = jnp.sum(jnp.where(hit & first, 1.0, 0.0), axis=1, keepdims=True)
    count1 = jnp.sum(jnp.where(hit & jnp.logical_not(first), 1.0, 0.0), axis=1, keepdims=True)
    count = jnp.where(row_list == 0, count0, count1)
    table = jnp.where(count > 0.5, jnp.log2(jnp.maximum(count, 1.0)), NEG)
    table_ref[...] = table
    biases = [tail_bias(row_list)] + tile_bias(table, 0, own)
    for copy in copies[4:]:
        copy.wait()
    for head in range(heads):
        cols = slice(head * WIDTH, (head + 1) * WIDTH)
        for pair in range(head * pairs // heads, (head + 1) * pairs // heads):
            s = add_tiles(dot_nt(k_ref[:, cols], pair_rows(q_ref, pair)), biases)
            top = jnp.max(s, axis=0, keepdims=True)
            p = jnp.exp2(s - top)
            d = dot_nt(v_ref[:, cols], pair_rows(g_ref, pair))
            at = slice(pair * PAIR, (pair + 1) * PAIR)
            here = columns(pair - head * pairs // heads, PAIR)
            p_ref[head, :, here] = p
            d_ref[head, :, here] = d
            stats_ref[0:1, at] = top
            stats_ref[1:2, at] = jnp.sum(p, axis=0, keepdims=True)
            stats_ref[2:3, at] = jnp.sum(p * d, axis=0, keepdims=True)


def far_key_kernel(
    unroll, q_ref, g_ref, k_ref, stats_ref, table_ref, back_ref, p_ref, fin_ref, low_ref
):
    far_tiles = k_ref.shape[0] // TILE
    heads = k_ref.shape[1] // WIDTH
    per_head = q_ref.shape[1] // PAIR // heads
    shifts, own_keys, _ = back_ref.shape
    biases = tile_bias(table_ref[...], own_keys // TILE, far_tiles)
    for head in range(heads):
        cols = slice(head * WIDTH, (head + 1) * WIDTH)

        def step(i):
            pair = head * per_head + i
            at = columns(pair, PAIR)
            here = columns(i, PAIR)
            s = add_tiles(dot_nt(k_ref[:, cols], pair_rows(q_ref, pair)), biases)
            near_top = stats_ref[0:1, at]
            top = jnp.maximum(near_top, jnp.max(s, axis=0, keepdims=True))
            p = jnp.exp2(s - top)
            fade = jnp.exp2(near_top - top)
            inverse = 1.0 / (stats_ref[1:2, at] * fade + jnp.sum(p, axis=0, keepdims=True))
            fade = fade * inverse
            fin_ref[0:1, at] = fade
            fin_ref[1:2, at] = stats_ref[2:3, at] * fade
            p = p * inverse
            p_ref[head, :, here] = p.astype(p_ref.dtype)
            low_ref[:, here] = p.astype(BF16)

        repeat(per_head, unroll, step)
        dv = dot_nn(low_ref[...], stacked_rows(g_ref, head, 2 * per_head)).astype(BF16)
        for shift in range(shifts):
            back_ref[shift, :, cols] = dv[shift * own_keys : (shift + 1) * own_keys]


def far_value_kernel(unroll, q_ref, g_ref, v_ref, p_ref, fin_ref, back_ref, ds_ref, delta_ref):
    heads = v_ref.shape[1] // WIDTH
    per_head = q_ref.shape[1] // PAIR // heads
    shifts, own_keys, _ = back_ref.shape
    for head in range(heads):
        cols = slice(head * WIDTH, (head + 1) * WIDTH)

        def step(i):
            pair = head * per_head + i
            at = columns(pair, PAIR)
            here = columns(i, PAIR)
            d = dot_nt(v_ref[:, cols], pair_rows(g_ref, pair))
            p = p_ref[head, :, here].astype(F32)
            delta = fin_ref[1:2, at] + jnp.sum(p * d, axis=0, keepdims=True)
            delta_ref[0:1, at] = delta
            ds_ref[head, :, here] = (p * (d - delta)).astype(BF16)

        repeat(per_head, unroll, step)
        dk = (dot_nn(ds_ref[head], stacked_rows(q_ref, head, 2 * per_head)) * SCALE).astype(BF16)
        for shift in range(shifts):
            back_ref[shift, :, cols] = dk[shift * own_keys : (shift + 1) * own_keys]


def last_kernel(
    unroll, q_ref, g_ref, k_ref, p_ref, d_ref, fin_ref, delta_ref, fk_ref, fds_ref,
    dq_ref, dtk_ref, dtv_ref, dok_ref, dov_ref, low_ref, ds_ref,
):
    tail = dtk_ref.shape[0]
    heads = k_ref.shape[1] // WIDTH
    per_head = q_ref.shape[1] // PAIR // heads
    for head in range(heads):
        cols = slice(head * WIDTH, (head + 1) * WIDTH)

        def step(i):
            pair = head * per_head + i
            at = columns(pair, PAIR)
            here = columns(i, PAIR)
            p = p_ref[head, :, here] * fin_ref[0:1, at]
            ds = (p * (d_ref[head, :, here] - delta_ref[0:1, at])).astype(BF16)
            low_ref[:, here] = p.astype(BF16)
            ds_ref[:, here] = ds
            dq = dot_tn(k_ref[:, cols], ds) + dot_tn(fk_ref[:, cols], fds_ref[head, :, here])
            dq = dq * SCALE
            dq = jnp.concatenate([dq[:, :WIDTH].T, dq[:, WIDTH:].T], axis=1)
            dq_ref[:, at] = dq.astype(BF16)

        repeat(per_head, unroll, step)
        dk = dot_nn(ds_ref[...], stacked_rows(q_ref, head, 2 * per_head)) * SCALE
        dv = dot_nn(low_ref[...], stacked_rows(g_ref, head, 2 * per_head))
        dtk_ref[:, cols] = dk[:tail].astype(BF16)
        dtv_ref[:, cols] = dv[:tail].astype(BF16)
        dok_ref[:, cols] = dk[tail:]
        dov_ref[:, cols] = dv[tail:]


def call(kernel, spaces, outs, scratch, flops, mib, *args):
    vmem = pl.BlockSpec(memory_space=pltpu.VMEM)
    moved = sum(a.size * a.dtype.itemsize for a in args) + sum(
        math.prod(o.shape) * o.dtype.itemsize for o in outs
    )
    return pl.pallas_call(
        kernel,
        out_shape=outs,
        in_specs=[pl.BlockSpec(memory_space=space) for space in spaces],
        out_specs=[vmem] * len(outs),
        scratch_shapes=scratch,
        compiler_params=pltpu.CompilerParams(vmem_limit_bytes=mib * 2**20),
        cost_estimate=pl.CostEstimate(flops=flops, bytes_accessed=moved, transcendentals=0),
    )(*args)


def body(q, g, tk, tv, ck, cv, row_list, read_owner, read_tile, read_list, read_count):
    ctx = lax.axis_size("ctx")
    rows, q_width = q.shape
    kv_width = tk.shape[1]
    heads = kv_width // WIDTH
    group_rows = rows * (q_width // kv_width)
    own_keys = ck.shape[0]
    own = own_keys // TILE
    far_keys = (ctx - 1) * own_keys
    near_keys = rows + own_keys
    slots = -(-ctx * own // 8) * 8
    unroll = ctx <= 2
    row_list = row_list.reshape(1, rows)

    def shifted(x, shift):
        return lax.ppermute(x, "ctx", [(o, (o - shift) % ctx) for o in range(ctx)])

    far_k = [shifted(ck, s) for s in range(1, ctx)]
    far_v = [shifted(cv, s) for s in range(1, ctx)]
    shape = jax.ShapeDtypeStruct
    product = 2 * q_width * rows * WIDTH
    small = read_owner.shape
    here = [
        pltpu.with_memory_space_constraint(a, pltpu.HBM)
        for a in (q, g, tk, tv, ck, cv, row_list, read_owner, read_tile, read_list)
    ]
    q, g, near_k, near_p, near_d, stats, table = call(
        functools.partial(near_kernel, ctx),
        [pltpu.HBM] * len(here) + [pltpu.SMEM],
        [
            shape(q.shape, BF16),
            shape(g.shape, BF16),
            shape((near_keys, kv_width), BF16),
            shape((heads, near_keys, group_rows), F32),
            shape((heads, near_keys, group_rows), F32),
            shape((8, heads * group_rows), F32),
            shape((slots, rows), F32),
        ],
        [
            pltpu.VMEM((near_keys, kv_width), BF16),
            pltpu.VMEM(row_list.shape, jnp.int32),
            pltpu.VMEM(small, jnp.int32),
            pltpu.VMEM(small, jnp.int32),
            pltpu.VMEM(small, jnp.int32),
            pltpu.SemaphoreType.DMA((10,)),
        ],
        2 * product * near_keys // WIDTH,
        32,
        *here, read_count,
    )
    mib = 32 if unroll else 60
    far_k = far_k[0] if ctx == 2 else jnp.concatenate(far_k, axis=0)
    back_v, far_p, fin = call(
        functools.partial(far_key_kernel, unroll),
        [pltpu.VMEM] * 5,
        [
            shape((ctx - 1, own_keys, kv_width), BF16),
            shape((heads, far_keys, group_rows), F32 if unroll else BF16),
            shape((8, heads * group_rows), F32),
        ],
        [pltpu.VMEM((far_keys, group_rows), BF16)],
        2 * product * far_keys // WIDTH,
        mib,
        q, g, far_k, stats, table,
    )
    returned_v = [shifted(back_v[s - 1], -s) for s in range(1, ctx)]
    far_v = far_v[0] if ctx == 2 else jnp.concatenate(far_v, axis=0)
    back_k, far_ds, delta = call(
        functools.partial(far_value_kernel, unroll),
        [pltpu.VMEM] * 5,
        [
            shape((ctx - 1, own_keys, kv_width), BF16),
            shape((heads, far_keys, group_rows), BF16),
            shape((8, heads * group_rows), F32),
        ],
        [],
        2 * product * far_keys // WIDTH,
        mib,
        q, g, far_v, far_p, fin,
    )
    returned_k = [shifted(back_k[s - 1], -s) for s in range(1, ctx)]
    dq, dtk, dtv, dok, dov = call(
        functools.partial(last_kernel, unroll),
        [pltpu.VMEM] * 9,
        [
            shape(q.shape, BF16),
            shape(tk.shape, BF16),
            shape(tv.shape, BF16),
            shape(ck.shape, F32),
            shape(cv.shape, F32),
        ],
        [pltpu.VMEM((near_keys, group_rows), BF16), pltpu.VMEM((near_keys, group_rows), BF16)],
        product * (3 * near_keys + far_keys) // WIDTH,
        mib,
        q, g, near_k, near_p, near_d, fin, delta, far_k, far_ds,
    )
    for key_block, value_block in zip(returned_k, returned_v):
        dok = dok + key_block.astype(F32)
        dov = dov + value_block.astype(F32)
    return dq, dtk, dtv, dok, dov


def solution(mesh):
    wide = P(("dp", "ctx"), "tp")
    lone = P(("dp", "ctx"))
    flat = P(("dp", "ctx"), None)
    return jax.shard_map(
        body,
        mesh=mesh,
        in_specs=(wide,) * 6 + (lone, flat, flat, flat, lone),
        out_specs=(wide,) * 5,
        check_vma=False,
    )
```

profile of v0, /device:TPU:0, one launch (start us, length us, event | category | flops | bytes accessed | tf_op | source)
XLA Modules:
  0.0 18.7 jit_solution(13360383834494139809)
XLA Ops:
  0.6 3.0 %collective-permute-start = (bf16[256,256]{1,0:T(8,128)(2,1)}, bf16[256,256]{1,0:T(8,128)(2,1)S(1)}, u32[]{:S(2)}, u32[]{:S(2)}) collective-permute-start(bf16[256,256]{1,0:T(8,128)(2,1)} %ok_in.1), channel_id=1, source_target_pairs={{0,16},{16,0},{1,17},{17,1},{2,18},{18,2},{3,19},{19,3},{4,20},{20... | collective-permute-start | bytes 393224 | tf_op jit(solution)/shard_map/ppermute | solution.py:261
  3.6 0.1 collective-permute-start.1
  4.4 2.9 %shard_map.146 = (bf16[128,2048]{1,0:T(8,128)(2,1)S(1)}, bf16[128,2048]{1,0:T(8,128)(2,1)S(1)}, bf16[384,256]{1,0:T(8,128)(2,1)S(1)}, f32[2,384,1024]{2,1,0:T(8,...) custom-call(bf16[128,2048]{1,0:T(8,128)(2,1)} %q_in.1, ...), custom_call_target="tpu_custom_call" | custom-call | flops 402653184 | bytes 9048868 | tf_op jit(solution)/shard_map/pallas_call | solution.py:235
  7.2 0.9 %collective-permute-done.k_ref.fk_ref = bf16[256,256]{1,0:T(8,128)(2,1)S(1)} collective-permute-done((bf16[256,256]{1,0:T(8,128)(2,1)}, bf16[256,256]{1,0:T(8,128)(2,1)S(1)}, u32[]{:S(2)}, u32[]{:S(2)}) %collective-permute-start) | collective-permute-done | bytes 131104 | tf_op jit(solution)/shard_map/ppermute | solution.py:261
  8.2 1.3 %shard_map.147 = (bf16[1,256,256]{2,1,0:T(8,128)(2,1)S(1)}, f32[2,256,1024]{2,1,0:T(8,128)S(1)}, f32[8,2048]{1,0:T(8,128)S(1)}) custom-call(bf16[128,2048]{1,0:T(8,128)(2,1)S(1)} %get-tuple-element.23.q_ref, bf16[128,2048]{1,0:T(8,128)(2,1)S(1)} %get-tuple-element.24.g_ref, bf16[256,256]{1,0:T(8,128)(2,1)S(1)} %collective-permute-done.k_ref.fk_ref, ...), custom_call_target="tpu_custom_call" | custom-call | flops 268435456 | bytes 3543040 | tf_op jit(solution)/shard_map/pallas_call | solution.py:235
  9.5 2.1 %collective-permute-start.3 = (bf16[256,256]{1,0:T(8,128)(2,1)S(1)}, bf16[256,256]{1,0:T(8,128)(2,1)S(1)}, u32[]{:S(2)}, u32[]{:S(2)}) collective-permute-start(bf16[256,256]{1,0:T(8,128)(2,1)S(1)} %bitcast.3), channel_id=1, source_target_pairs={{0,16},{16,0},{1,17},{17,1},{2,18},{18,2},{3,19},{19,3},{4,20},{20... | collective-permute-start | bytes 393224 | tf_op jit(solution)/shard_map/ppermute | solution.py:261
  11.7 0.0 collective-permute-done.1.v_ref
  11.7 1.3 %shard_map.148 = (bf16[1,256,256]{2,1,0:T(8,128)(2,1)S(1)}, bf16[2,256,1024]{2,1,0:T(8,128)(2,1)S(1)}, f32[8,2048]{1,0:T(8,128)S(1)}) custom-call(bf16[128,2048]{1,0:T(8,128)(2,1)S(1)} %get-tuple-element.23.q_ref, bf16[128,2048]{1,0:T(8,128)(2,1)S(1)} %get-tuple-element.24.g_ref, bf16[256,256]{1,0:T(8,128)(2,1)S(1)} %collective-permute-done.1.v_ref, ...), custom_call_target="tpu_custom_call" | custom-call | flops 268435456 | bytes 4587520 | tf_op jit(solution)/shard_map/pallas_call | solution.py:235
  12.9 0.3 %collective-permute-start.2 = (bf16[256,256]{1,0:T(8,128)(2,1)S(1)}, bf16[256,256]{1,0:T(8,128)(2,1)S(1)}, u32[]{:S(2)}, u32[]{:S(2)}) collective-permute-start(bf16[256,256]{1,0:T(8,128)(2,1)S(1)} %bitcast.4), channel_id=1, source_target_pairs={{0,16},{16,0},{1,17},{17,1},{2,18},{18,2},{3,19},{19,3},{4,20},{20... | collective-permute-start | bytes 393224 | tf_op jit(solution)/shard_map/ppermute | solution.py:261
  13.2 2.3 %shard_map.149 = (bf16[128,2048]{1,0:T(8,128)(2,1)}, bf16[128,256]{1,0:T(8,128)(2,1)}, bf16[128,256]{1,0:T(8,128)(2,1)}, f32[256,256]{1,0:T(8,128)S(1)}, f32[256,256]{1,0:T(8,128)S(1)}) custom-call(bf16[128,2048]{1,0:T(8,128)(2,1)S(1)} %get-tuple-element.23.q_ref, bf16[128,2048]{1,0:T(8,128)(2,1)S(1)} %get-tuple-element.24.g_ref, ...), custom_call_target="tpu_custom_call" | custom-call | flops 738197504 | bytes 10027008 | tf_op jit(solution)/shard_map/pallas_call | solution.py:235
  15.5 0.3 %collective-permute-done.3 = bf16[256,256]{1,0:T(8,128)(2,1)S(1)} collective-permute-done((bf16[256,256]{1,0:T(8,128)(2,1)S(1)}, bf16[256,256]{1,0:T(8,128)(2,1)S(1)}, u32[]{:S(2)}, u32[]{:S(2)}) %collective-permute-start.3) | collective-permute-done | bytes 131104 | tf_op jit(solution)/shard_map/ppermute | solution.py:261
  15.7 0.7 %convert_add_fusion = f32[256,256]{1,0:T(8,128)} fusion(f32[256,256]{1,0:T(8,128)S(1)} %get-tuple-element.39, bf16[256,256]{1,0:T(8,128)(2,1)S(1)} %collective-permute-done.3), kind=kLoop, calls=%fused_computation | loop fusion | flops 131072 | bytes 655360 | tf_op jit(solution)/shard_map/add | solution.py:344
  16.5 1.5 %collective-permute-done.2 = bf16[256,256]{1,0:T(8,128)(2,1)S(1)} collective-permute-done((bf16[256,256]{1,0:T(8,128)(2,1)S(1)}, bf16[256,256]{1,0:T(8,128)(2,1)S(1)}, u32[]{:S(2)}, u32[]{:S(2)}) %collective-permute-start.2) | collective-permute-done | bytes 131104 | tf_op jit(solution)/shard_map/ppermute | solution.py:261
  17.9 0.7 %convert_add_fusion.1 = f32[256,256]{1,0:T(8,128)} fusion(f32[256,256]{1,0:T(8,128)S(1)} %get-tuple-element.37, bf16[256,256]{1,0:T(8,128)(2,1)S(1)} %collective-permute-done.2), kind=kLoop, calls=%fused_computation.1 | loop fusion | flops 131072 | bytes 655360 | tf_op jit(solution)/shard_map/add | solution.py:343
Async XLA Ops:
  0.6 7.5 %collective-permute-start = (bf16[256,256]{1,0:T(8,128)(2,1)}, bf16[256,256]{1,0:T(8,128)(2,1)S(1)}, u32[]{:S(2)}, u32[]{:S(2)}) collective-permute-start(bf16[256,256]{1,0:T(8,128)(2,1)} %ok_in.1), channel_id=1, source_target_pairs={{0,16},{16,0},{1,17},{17,1},{2,18},{18,2},{3,19},{19,3},{4,20},{20... | collective-permute-start | bytes 393224 | tf_op jit(solution)/shard_map/ppermute | solution.py:261
  3.6 8.0 %collective-permute-start.1 = (bf16[256,256]{1,0:T(8,128)(2,1)}, bf16[256,256]{1,0:T(8,128)(2,1)S(1)}, u32[]{:S(2)}, u32[]{:S(2)}) collective-permute-start(bf16[256,256]{1,0:T(8,128)(2,1)} %ov_in.1), channel_id=1, source_target_pairs={{0,16},{16,0},{1,17},{17,1},{2,18},{18,2},{3,19},{19,3},{4,20},{20... | collective-permute-start | bytes 393224 | tf_op jit(solution)/shard_map/ppermute | solution.py:261
  9.5 6.2 %collective-permute-start.3 = (bf16[256,256]{1,0:T(8,128)(2,1)S(1)}, bf16[256,256]{1,0:T(8,128)(2,1)S(1)}, u32[]{:S(2)}, u32[]{:S(2)}) collective-permute-start(bf16[256,256]{1,0:T(8,128)(2,1)S(1)} %bitcast.3), channel_id=1, source_target_pairs={{0,16},{16,0},{1,17},{17,1},{2,18},{18,2},{3,19},{19,3},{4,20},{20... | collective-permute-start | bytes 393224 | tf_op jit(solution)/shard_map/ppermute | solution.py:261
  12.9 5.0 %collective-permute-start.2 = (bf16[256,256]{1,0:T(8,128)(2,1)S(1)}, bf16[256,256]{1,0:T(8,128)(2,1)S(1)}, u32[]{:S(2)}, u32[]{:S(2)}) collective-permute-start(bf16[256,256]{1,0:T(8,128)(2,1)S(1)} %bitcast.4), channel_id=1, source_target_pairs={{0,16},{16,0},{1,17},{17,1},{2,18},{18,2},{3,19},{19,3},{4,20},{20... | collective-permute-start | bytes 393224 | tf_op jit(solution)/shard_map/ppermute | solution.py:261
where the time goes:
time: 18.8 us; the launch traced here: 18.7 us
  Pallas kernels  7.75 us (41%)
  starting transfers between devices  5.51 us (29%)
  waiting for transfers between devices  2.65 us (14%)
  other arithmetic  1.45 us (8%)
  between operations  1.31 us (7%)
    pallas_call x4, Pallas kernels, call(): pl.pallas_call(kernel, out_shape=outs, in_specs=[pl.BlockSpec(memory_spac...  7.75 us
    ppermute x4, starting transfers between devices, shifted(): return lax.ppermute(x, 'ctx', [(o, (o - shift) % ctx) for o in range(ctx)])  5.51 us
    ppermute x4, waiting for transfers between devices, shifted(): return lax.ppermute(x, 'ctx', [(o, (o - shift) % ctx) for o in range(ctx)])  2.65 us
    add x1, other arithmetic, body(): dov = dov + value_block.astype(F32)  0.73 us
    add x1, other arithmetic, body(): dok = dok + key_block.astype(F32)  0.73 us
  transfers between devices with their start and end apart: 4, of which 3 were waited for; matrix products, arithmetic and copies ran while one was open for 4% of the time, Pallas kernels for 41%

commit v1 on v0

--- a/solution.py
+++ b/solution.py
@@ -138,9 +138,31 @@
             stats_ref[2:3, at] = jnp.sum(p * d, axis=0, keepdims=True)
 
 
+def load_far(all_ref, far_ref, sems):
+    keys = all_ref.shape[0] - far_ref.shape[0]
+    shifts = far_ref.shape[0] // keys
+    ctx = shifts + 1
+    me = lax.axis_index("ctx")
+    copies = []
+    for shift in range(shifts):
+        owner = lax.rem(me + shift + 1, ctx)
+        copies.append(
+            pltpu.make_async_copy(
+                all_ref.at[pl.ds(pl.multiple_of(owner * keys, keys), keys)],
+                far_ref.at[shift * keys : (shift + 1) * keys],
+                sems.at[shift],
+            )
+        )
+    for copy in copies:
+        copy.start()
+    for copy in copies:
+        copy.wait()
+
+
 def far_key_kernel(
-    unroll, q_ref, g_ref, k_ref, stats_ref, table_ref, back_ref, p_ref, fin_ref, low_ref
+    unroll, q_ref, g_ref, all_ref, stats_ref, table_ref, back_ref, p_ref, fin_ref, k_ref, low_ref, sems
 ):
+    load_far(all_ref, k_ref, sems)
     far_tiles = k_ref.shape[0] // TILE
     heads = k_ref.shape[1] // WIDTH
     per_head = q_ref.shape[1] // PAIR // heads
@@ -172,7 +194,10 @@
             back_ref[shift, :, cols] = dv[shift * own_keys : (shift + 1) * own_keys]
 
 
-def far_value_kernel(unroll, q_ref, g_ref, v_ref, p_ref, fin_ref, back_ref, ds_ref, delta_ref):
+def far_value_kernel(
+    unroll, q_ref, g_ref, all_ref, p_ref, fin_ref, back_ref, ds_ref, delta_ref, v_ref, sems
+):
+    load_far(all_ref, v_ref, sems)
     heads = v_ref.shape[1] // WIDTH
     per_head = q_ref.shape[1] // PAIR // heads
     shifts, own_keys, _ = back_ref.shape
@@ -260,8 +285,8 @@
     def shifted(x, shift):
         return lax.ppermute(x, "ctx", [(o, (o - shift) % ctx) for o in range(ctx)])
 
-    far_k = [shifted(ck, s) for s in range(1, ctx)]
-    far_v = [shifted(cv, s) for s in range(1, ctx)]
+    all_k = lax.all_gather(ck, "ctx", axis=0, tiled=True)
+    all_v = lax.all_gather(cv, "ctx", axis=0, tiled=True)
     shape = jax.ShapeDtypeStruct
     product = 2 * q_width * rows * WIDTH
     small = read_owner.shape
@@ -294,34 +319,33 @@
         *here, read_count,
     )
     mib = 32 if unroll else 60
-    far_k = far_k[0] if ctx == 2 else jnp.concatenate(far_k, axis=0)
-    back_v, far_p, fin = call(
+    back_v, far_p, fin, far_k = call(
         functools.partial(far_key_kernel, unroll),
-        [pltpu.VMEM] * 5,
+        [pltpu.VMEM, pltpu.VMEM, pltpu.HBM, pltpu.VMEM, pltpu.VMEM],
         [
             shape((ctx - 1, own_keys, kv_width), BF16),
             shape((heads, far_keys, group_rows), F32 if unroll else BF16),
             shape((8, heads * group_rows), F32),
-        ],
-        [pltpu.VMEM((far_keys, group_rows), BF16)],
+            shape((far_keys, kv_width), BF16),
+        ],
+        [pltpu.VMEM((far_keys, group_rows), BF16), pltpu.SemaphoreType.DMA((ctx - 1,))],
         2 * product * far_keys // WIDTH,
         mib,
-        q, g, far_k, stats, table,
+        q, g, pltpu.with_memory_space_constraint(all_k, pltpu.HBM), stats, table,
     )
     returned_v = [shifted(back_v[s - 1], -s) for s in range(1, ctx)]
-    far_v = far_v[0] if ctx == 2 else jnp.concatenate(far_v, axis=0)
     back_k, far_ds, delta = call(
         functools.partial(far_value_kernel, unroll),
-        [pltpu.VMEM] * 5,
+        [pltpu.VMEM, pltpu.VMEM, pltpu.HBM, pltpu.VMEM, pltpu.VMEM],
         [
             shape((ctx - 1, own_keys, kv_width), BF16),
             shape((heads, far_keys, group_rows), BF16),
             shape((8, heads * group_rows), F32),
         ],
-        [],
+        [pltpu.VMEM((far_keys, kv_width), BF16), pltpu.SemaphoreType.DMA((ctx - 1,))],
         2 * product * far_keys // WIDTH,
         mib,
-        q, g, far_v, far_p, fin,
+        q, g, pltpu.with_memory_space_constraint(all_v, pltpu.HBM), far_p, fin,
     )
     returned_k = [shifted(back_k[s - 1], -s) for s in range(1, ctx)]
     dq, dtk, dtv, dok, dov = call(

time: 18.8 us -> 31.1 us (1.65)
  blocking collectives: 0 us -> 14.9 us
  starting transfers between devices: 5.51 us -> 2.09 us
  Pallas kernels: 7.75 us -> 9.6 us
  waiting for transfers between devices: 2.65 us -> 1.45 us
    all_gather x0 -> x2, blocking collectives: none -> 14.9 us  [the longest x1 8.96 us: body(): all_k = lax.all_gather(ck, 'ctx', axis=0, tiled=True)]
    ppermute x4 -> x2, starting transfers between devices: 5.51 us -> 2.09 us  [shifted(): return lax.ppermute(x, 'ctx', [(o, (o - shift) % ctx) for o in range(ctx)])]
    pallas_call x4, Pallas kernels: 7.75 us -> 9.6 us  [call(): pl.pallas_call(kernel, out_shape=outs, in_specs=[pl.BlockSpec(memory_spac...]
    ppermute x4 -> x2, waiting for transfers between devices: 2.65 us -> 1.45 us  [shifted(): return lax.ppermute(x, 'ctx', [(o, (o - shift) % ctx) for o in range(ctx)])]
  transfers between devices with their start and end apart: 4 -> 2, of which waited for: 3 -> 2; matrix products, arithmetic and copies ran while one was open for 4% -> 2% of each run, Pallas kernels for 41% -> 7%
where the time goes in v1:
time: 31.1 us; the launch traced here: 30.8 us
  blocking collectives  14.9 us (48%)
  Pallas kernels  9.6 us (31%)
  starting transfers between devices  2.09 us (7%)
  other arithmetic  1.47 us (5%)
  waiting for transfers between devices  1.45 us (5%)
  between operations  1.31 us (4%)
    pallas_call x4, Pallas kernels, call(): pl.pallas_call(kernel, out_shape=outs, in_specs=[pl.BlockSpec(memory_spac...  9.6 us
    all_gather x1, blocking collectives, body(): all_k = lax.all_gather(ck, 'ctx', axis=0, tiled=True)  8.96 us
    all_gather x1, blocking collectives, body(): all_v = lax.all_gather(cv, 'ctx', axis=0, tiled=True)  5.95 us
    ppermute x2, starting transfers between devices, shifted(): return lax.ppermute(x, 'ctx', [(o, (o - shift) % ctx) for o in range(ctx)])  2.09 us
    ppermute x2, waiting for transfers between devices, shifted(): return lax.ppermute(x, 'ctx', [(o, (o - shift) % ctx) for o in range(ctx)])  1.45 us
    add x1, other arithmetic, body(): dok = dok + key_block.astype(F32)  0.73 us
    add x1, other arithmetic, body(): dov = dov + value_block.astype(F32)  0.73 us
  transfers between devices with their start and end apart: 2, of which 2 were waited for; matrix products, arithmetic and copies ran while one was open for 2% of the time, Pallas kernels for 7%

profile of v1, /device:TPU:0, one launch (start us, length us, event | category | flops | bytes accessed | tf_op | source)
XLA Modules:
  0.0 30.8 jit_solution(8088848697913680912)
XLA Ops:
  1.3 9.0 %all_gather.6.all_ref = bf16[512,256]{1,0:T(8,128)(2,1)} all-gather(bf16[256,256]{1,0:T(8,128)(2,1)} %ok_in.1), channel_id=1, replica_groups=mesh['ctx'=2,'tp'=4,'dp'=4] {'ctx'}, dimensions={0}, use_global_device_ids=true | all-gather | bytes 393216 | tf_op jit(solution)/shard_map/all_gather | solution.py:288
  10.2 5.9 %all_gather.7.all_ref = bf16[512,256]{1,0:T(8,128)(2,1)} all-gather(bf16[256,256]{1,0:T(8,128)(2,1)} %ov_in.1), channel_id=1, replica_groups=mesh['ctx'=2,'tp'=4,'dp'=4] {'ctx'}, dimensions={0}, use_global_device_ids=true | all-gather | bytes 393216 | tf_op jit(solution)/shard_map/all_gather | solution.py:289
  16.2 2.9 %shard_map.146 = (bf16[128,2048]{1,0:T(8,128)(2,1)S(1)}, bf16[128,2048]{1,0:T(8,128)(2,1)S(1)}, bf16[384,256]{1,0:T(8,128)(2,1)S(1)}, f32[2,384,1024]{2,1,0:T(8,...) custom-call(bf16[128,2048]{1,0:T(8,128)(2,1)} %q_in.1, ...), custom_call_target="tpu_custom_call" | custom-call | flops 402653184 | bytes 9048868 | tf_op jit(solution)/shard_map/pallas_call | solution.py:260
  19.1 2.3 %shard_map.147 = (bf16[1,256,256]{2,1,0:T(8,128)(2,1)S(1)}, f32[2,256,1024]{2,1,0:T(8,128)S(1)}, f32[8,2048]{1,0:T(8,128)S(1)}, bf16[256,256]{1,0:T(8,128)(2,1)S(1)}) custom-call(bf16[128,2048]{1,0:T(8,128)(2,1)S(1)} %get-tuple-element.24.q_ref, bf16[128,2048]{1,0:T(8,128)(2,1)S(1)} %get-tuple-element.25.g_ref, bf16[512,256]{1,0:T(8,128)(2,1)} %all_gather.6.all_ref, ...), custom_call_target="tpu_custom_call" | custom-call | flops 268435456 | bytes 3805184 | tf_op jit(solution)/shard_map/pallas_call | solution.py:260
  21.3 2.2 %shard_map.148 = (bf16[1,256,256]{2,1,0:T(8,128)(2,1)S(1)}, bf16[2,256,1024]{2,1,0:T(8,128)(2,1)S(1)}, f32[8,2048]{1,0:T(8,128)S(1)}) custom-call(bf16[128,2048]{1,0:T(8,128)(2,1)S(1)} %get-tuple-element.24.q_ref, bf16[128,2048]{1,0:T(8,128)(2,1)S(1)} %get-tuple-element.25.g_ref, bf16[512,256]{1,0:T(8,128)(2,1)} %all_gather.7.all_ref, ...), custom_call_target="tpu_custom_call" | custom-call | flops 268435456 | bytes 4718592 | tf_op jit(solution)/shard_map/pallas_call | solution.py:260
  23.5 1.6 %collective-permute-start = (bf16[256,256]{1,0:T(8,128)(2,1)S(1)}, bf16[256,256]{1,0:T(8,128)(2,1)S(1)}, u32[]{:S(2)}, u32[]{:S(2)}) collective-permute-start(bf16[256,256]{1,0:T(8,128)(2,1)S(1)} %bitcast.4), channel_id=1, source_target_pairs={{0,16},{16,0},{1,17},{17,1},{2,18},{18,2},{3,19},{19,3},{4,20},{20... | collective-permute-start | bytes 393224 | tf_op jit(solution)/shard_map/ppermute | solution.py:286
  25.1 0.5 %collective-permute-start.1 = (bf16[256,256]{1,0:T(8,128)(2,1)S(1)}, bf16[256,256]{1,0:T(8,128)(2,1)S(1)}, u32[]{:S(2)}, u32[]{:S(2)}) collective-permute-start(bf16[256,256]{1,0:T(8,128)(2,1)S(1)} %bitcast.3), channel_id=1, source_target_pairs={{0,16},{16,0},{1,17},{17,1},{2,18},{18,2},{3,19},{19,3},{4,20},{20... | collective-permute-start | bytes 393224 | tf_op jit(solution)/shard_map/ppermute | solution.py:286
  25.6 2.3 %shard_map.149 = (bf16[128,2048]{1,0:T(8,128)(2,1)}, bf16[128,256]{1,0:T(8,128)(2,1)}, bf16[128,256]{1,0:T(8,128)(2,1)}, f32[256,256]{1,0:T(8,128)S(1)}, f32[256,256]{1,0:T(8,128)S(1)}) custom-call(bf16[128,2048]{1,0:T(8,128)(2,1)S(1)} %get-tuple-element.24.q_ref, bf16[128,2048]{1,0:T(8,128)(2,1)S(1)} %get-tuple-element.25.g_ref, ...), custom_call_target="tpu_custom_call" | custom-call | flops 738197504 | bytes 10027008 | tf_op jit(solution)/shard_map/pallas_call | solution.py:260
  27.9 0.8 %collective-permute-done = bf16[256,256]{1,0:T(8,128)(2,1)S(1)} collective-permute-done((bf16[256,256]{1,0:T(8,128)(2,1)S(1)}, bf16[256,256]{1,0:T(8,128)(2,1)S(1)}, u32[]{:S(2)}, u32[]{:S(2)}) %collective-permute-start) | collective-permute-done | bytes 131104 | tf_op jit(solution)/shard_map/ppermute | solution.py:286
  28.7 0.7 %convert_add_fusion.1 = f32[256,256]{1,0:T(8,128)} fusion(f32[256,256]{1,0:T(8,128)S(1)} %get-tuple-element.39, bf16[256,256]{1,0:T(8,128)(2,1)S(1)} %collective-permute-done), kind=kLoop, calls=%fused_computation.1 | loop fusion | flops 131072 | bytes 655360 | tf_op jit(solution)/shard_map/add | solution.py:367
  29.4 0.7 %collective-permute-done.1 = bf16[256,256]{1,0:T(8,128)(2,1)S(1)} collective-permute-done((bf16[256,256]{1,0:T(8,128)(2,1)S(1)}, bf16[256,256]{1,0:T(8,128)(2,1)S(1)}, u32[]{:S(2)}, u32[]{:S(2)}) %collective-permute-start.1) | collective-permute-done | bytes 131104 | tf_op jit(solution)/shard_map/ppermute | solution.py:286
  30.1 0.7 %convert_add_fusion = f32[256,256]{1,0:T(8,128)} fusion(f32[256,256]{1,0:T(8,128)S(1)} %get-tuple-element.41, bf16[256,256]{1,0:T(8,128)(2,1)S(1)} %collective-permute-done.1), kind=kLoop, calls=%fused_computation | loop fusion | flops 131072 | bytes 655360 | tf_op jit(solution)/shard_map/add | solution.py:368
Async XLA Ops:
  23.5 5.1 %collective-permute-start = (bf16[256,256]{1,0:T(8,128)(2,1)S(1)}, bf16[256,256]{1,0:T(8,128)(2,1)S(1)}, u32[]{:S(2)}, u32[]{:S(2)}) collective-permute-start(bf16[256,256]{1,0:T(8,128)(2,1)S(1)} %bitcast.4), channel_id=1, source_target_pairs={{0,16},{16,0},{1,17},{17,1},{2,18},{18,2},{3,19},{19,3},{4,20},{20... | collective-permute-start | bytes 393224 | tf_op jit(solution)/shard_map/ppermute | solution.py:286
  25.1 5.0 %collective-permute-start.1 = (bf16[256,256]{1,0:T(8,128)(2,1)S(1)}, bf16[256,256]{1,0:T(8,128)(2,1)S(1)}, u32[]{:S(2)}, u32[]{:S(2)}) collective-permute-start(bf16[256,256]{1,0:T(8,128)(2,1)S(1)} %bitcast.3), channel_id=1, source_target_pairs={{0,16},{16,0},{1,17},{17,1},{2,18},{18,2},{3,19},{19,3},{4,20},{20... | collective-permute-start | bytes 393224 | tf_op jit(solution)/shard_map/ppermute | solution.py:286

commit v2 on v0

--- a/solution.py
+++ b/solution.py
@@ -41,6 +41,19 @@
             return carry
 
         lax.fori_loop(0, steps, one, 0)
+
+
+def added(steps, unroll, step, total_ref):
+    if unroll:
+        return functools.reduce(jnp.add, [step(i) for i in range(steps)])
+    (total_ref,) = total_ref
+    total_ref[...] = jnp.zeros_like(total_ref)
+
+    def one(i):
+        total_ref[...] += step(i)
+
+    repeat(steps, unroll, one)
+    return total_ref[...]
 
 
 def columns(i, width):
@@ -139,7 +152,7 @@
 
 
 def far_key_kernel(
-    unroll, q_ref, g_ref, k_ref, stats_ref, table_ref, back_ref, p_ref, fin_ref, low_ref
+    unroll, q_ref, g_ref, k_ref, stats_ref, table_ref, back_ref, p_ref, fin_ref, *total_ref
 ):
     far_tiles = k_ref.shape[0] // TILE
     heads = k_ref.shape[1] // WIDTH
@@ -162,17 +175,18 @@
             fade = fade * inverse
             fin_ref[0:1, at] = fade
             fin_ref[1:2, at] = stats_ref[2:3, at] * fade
-            p = p * inverse
-            p_ref[head, :, here] = p.astype(p_ref.dtype)
-            low_ref[:, here] = p.astype(BF16)
-
-        repeat(per_head, unroll, step)
-        dv = dot_nn(low_ref[...], stacked_rows(g_ref, head, 2 * per_head)).astype(BF16)
+            p = (p * inverse).astype(BF16)
+            p_ref[head, :, here] = p
+            return dot_nn(p, pair_rows(g_ref, pair))
+
+        dv = added(per_head, unroll, step, total_ref).astype(BF16)
         for shift in range(shifts):
             back_ref[shift, :, cols] = dv[shift * own_keys : (shift + 1) * own_keys]
 
 
-def far_value_kernel(unroll, q_ref, g_ref, v_ref, p_ref, fin_ref, back_ref, ds_ref, delta_ref):
+def far_value_kernel(
+    unroll, q_ref, g_ref, v_ref, p_ref, fin_ref, back_ref, ds_ref, delta_ref, *total_ref
+):
     heads = v_ref.shape[1] // WIDTH
     per_head = q_ref.shape[1] // PAIR // heads
     shifts, own_keys, _ = back_ref.shape
@@ -187,10 +201,11 @@
             p = p_ref[head, :, here].astype(F32)
             delta = fin_ref[1:2, at] + jnp.sum(p * d, axis=0, keepdims=True)
             delta_ref[0:1, at] = delta
-            ds_ref[head, :, here] = (p * (d - delta)).astype(BF16)
-
-        repeat(per_head, unroll, step)
-        dk = (dot_nn(ds_ref[head], stacked_rows(q_ref, head, 2 * per_head)) * SCALE).astype(BF16)
+            ds = (p * (d - delta)).astype(BF16)
+            ds_ref[head, :, here] = ds
+            return dot_nn(ds, pair_rows(q_ref, pair))
+
+        dk = (added(per_head, unroll, step, total_ref) * SCALE).astype(BF16)
         for shift in range(shifts):
             back_ref[shift, :, cols] = dk[shift * own_keys : (shift + 1) * own_keys]
 
@@ -211,16 +226,16 @@
             here = columns(i, PAIR)
             p = p_ref[head, :, here] * fin_ref[0:1, at]
             ds = (p * (d_ref[head, :, here] - delta_ref[0:1, at])).astype(BF16)
-            low_ref[:, here] = p.astype(BF16)
-            ds_ref[:, here] = ds
+            low_ref[head, :, here] = p.astype(BF16)
+            ds_ref[head, :, here] = ds
             dq = dot_tn(k_ref[:, cols], ds) + dot_tn(fk_ref[:, cols], fds_ref[head, :, here])
             dq = dq * SCALE
             dq = jnp.concatenate([dq[:, :WIDTH].T, dq[:, WIDTH:].T], axis=1)
             dq_ref[:, at] = dq.astype(BF16)
 
         repeat(per_head, unroll, step)
-        dk = dot_nn(ds_ref[...], stacked_rows(q_ref, head, 2 * per_head)) * SCALE
-        dv = dot_nn(low_ref[...], stacked_rows(g_ref, head, 2 * per_head))
+        dk = dot_nn(ds_ref[head], stacked_rows(q_ref, head, 2 * per_head)) * SCALE
+        dv = dot_nn(low_ref[head], stacked_rows(g_ref, head, 2 * per_head))
         dtk_ref[:, cols] = dk[:tail].astype(BF16)
         dtv_ref[:, cols] = dv[:tail].astype(BF16)
         dok_ref[:, cols] = dk[tail:]
@@ -294,16 +309,17 @@
         *here, read_count,
     )
     mib = 32 if unroll else 60
+    total = [] if unroll else [pltpu.VMEM((far_keys, WIDTH), F32)]
     far_k = far_k[0] if ctx == 2 else jnp.concatenate(far_k, axis=0)
     back_v, far_p, fin = call(
         functools.partial(far_key_kernel, unroll),
         [pltpu.VMEM] * 5,
         [
             shape((ctx - 1, own_keys, kv_width), BF16),
-            shape((heads, far_keys, group_rows), F32 if unroll else BF16),
+            shape((heads, far_keys, group_rows), BF16),
             shape((8, heads * group_rows), F32),
         ],
-        [pltpu.VMEM((far_keys, group_rows), BF16)],
+        total,
         2 * product * far_keys // WIDTH,
         mib,
         q, g, far_k, stats, table,
@@ -318,7 +334,7 @@
             shape((heads, far_keys, group_rows), BF16),
             shape((8, heads * group_rows), F32),
         ],
-        [],
+        total,
         2 * product * far_keys // WIDTH,
         mib,
         q, g, far_v, far_p, fin,
@@ -334,7 +350,7 @@
             shape(ck.shape, F32),
             shape(cv.shape, F32),
         ],
-        [pltpu.VMEM((near_keys, group_rows), BF16), pltpu.VMEM((near_keys, group_rows), BF16)],
+        [pltpu.VMEM((heads, near_keys, group_rows), BF16)] * 2,
         product * (3 * near_keys + far_keys) // WIDTH,
         mib,
         q, g, near_k, near_p, near_d, fin, delta, far_k, far_ds,

time: 18.8 us -> 19.7 us (1.048)
  waiting for transfers between devices: 2.65 us -> 4.22 us
  starting transfers between devices: 5.51 us -> 5.17 us
  Pallas kernels: 7.75 us -> 7.42 us
    ppermute x4, waiting for transfers between devices: 2.65 us -> 4.22 us  [shifted(): return lax.ppermute(x, 'ctx', [(o, (o - shift) % ctx) for o in range(ctx)])]
    ppermute x4, starting transfers between devices: 5.51 us -> 5.17 us  [shifted(): return lax.ppermute(x, 'ctx', [(o, (o - shift) % ctx) for o in range(ctx)])]
    pallas_call x4, Pallas kernels: 7.75 us -> 7.42 us  [call(): pl.pallas_call(kernel, out_shape=outs, in_specs=[pl.BlockSpec(memory_spac...]
  transfers between devices with their start and end apart: 4 -> 4, of which waited for: 3 -> 4; matrix products, arithmetic and copies ran while one was open for 4% -> 4% of each run, Pallas kernels for 41% -> 32%
where the time goes in v2:
time: 19.7 us; the launch traced here: 19.6 us
  Pallas kernels  7.42 us (38%)
  starting transfers between devices  5.17 us (26%)
  waiting for transfers between devices  4.22 us (21%)
  other arithmetic  1.45 us (7%)
  between operations  1.31 us (7%)
    pallas_call x4, Pallas kernels, call(): pl.pallas_call(kernel, out_shape=outs, in_specs=[pl.BlockSpec(memory_spac...  7.42 us
    ppermute x4, starting transfers between devices, shifted(): return lax.ppermute(x, 'ctx', [(o, (o - shift) % ctx) for o in range(ctx)])  5.17 us
    ppermute x4, waiting for transfers between devices, shifted(): return lax.ppermute(x, 'ctx', [(o, (o - shift) % ctx) for o in range(ctx)])  4.22 us
    add x1, other arithmetic, body(): dok = dok + key_block.astype(F32)  0.73 us
    add x1, other arithmetic, body(): dov = dov + value_block.astype(F32)  0.73 us
  transfers between devices with their start and end apart: 4, of which 4 were waited for; matrix products, arithmetic and copies ran while one was open for 4% of the time, Pallas kernels for 32%

profile of v2, /device:TPU:0, one launch (start us, length us, event | category | flops | bytes accessed | tf_op | source)
XLA Modules:
  0.0 19.6 jit_solution(15170678882944345693)
XLA Ops:
  0.6 3.0 %collective-permute-start = (bf16[256,256]{1,0:T(8,128)(2,1)}, bf16[256,256]{1,0:T(8,128)(2,1)S(1)}, u32[]{:S(2)}, u32[]{:S(2)}) collective-permute-start(bf16[256,256]{1,0:T(8,128)(2,1)} %ok_in.1), channel_id=1, source_target_pairs={{0,16},{16,0},{1,17},{17,1},{2,18},{18,2},{3,19},{19,3},{4,20},{20... | collective-permute-start | bytes 393224 | tf_op jit(solution)/shard_map/ppermute | solution.py:276
  3.6 0.1 collective-permute-start.1
  4.4 2.9 %shard_map.146 = (bf16[128,2048]{1,0:T(8,128)(2,1)S(1)}, bf16[128,2048]{1,0:T(8,128)(2,1)S(1)}, bf16[384,256]{1,0:T(8,128)(2,1)S(1)}, f32[2,384,1024]{2,1,0:T(8,...) custom-call(bf16[128,2048]{1,0:T(8,128)(2,1)} %q_in.1, ...), custom_call_target="tpu_custom_call" | custom-call | flops 402653184 | bytes 9048868 | tf_op jit(solution)/shard_map/pallas_call | solution.py:250
  7.2 0.9 %collective-permute-done.k_ref.fk_ref = bf16[256,256]{1,0:T(8,128)(2,1)S(1)} collective-permute-done((bf16[256,256]{1,0:T(8,128)(2,1)}, bf16[256,256]{1,0:T(8,128)(2,1)S(1)}, u32[]{:S(2)}, u32[]{:S(2)}) %collective-permute-start) | collective-permute-done | bytes 131104 | tf_op jit(solution)/shard_map/ppermute | solution.py:276
  8.2 1.2 %shard_map.147 = (bf16[1,256,256]{2,1,0:T(8,128)(2,1)S(1)}, bf16[2,256,1024]{2,1,0:T(8,128)(2,1)S(1)}, f32[8,2048]{1,0:T(8,128)S(1)}) custom-call(bf16[128,2048]{1,0:T(8,128)(2,1)S(1)} %get-tuple-element.23.q_ref, bf16[128,2048]{1,0:T(8,128)(2,1)S(1)} %get-tuple-element.24.g_ref, bf16[256,256]{1,0:T(8,128)(2,1)S(1)} %collective-permute-done.k_ref.fk_ref, ...), custom_call_target="tpu_custom_call" | custom-call | flops 268435456 | bytes 2494464 | tf_op jit(solution)/shard_map/pallas_call | solution.py:250
  9.3 0.8 %collective-permute-done.1.v_ref = bf16[256,256]{1,0:T(8,128)(2,1)S(1)} collective-permute-done((bf16[256,256]{1,0:T(8,128)(2,1)}, bf16[256,256]{1,0:T(8,128)(2,1)S(1)}, u32[]{:S(2)}, u32[]{:S(2)}) %collective-permute-start.1) | collective-permute-done | bytes 131104 | tf_op jit(solution)/shard_map/ppermute | solution.py:276
  10.2 1.1 %shard_map.148 = (bf16[1,256,256]{2,1,0:T(8,128)(2,1)S(1)}, bf16[2,256,1024]{2,1,0:T(8,128)(2,1)S(1)}, f32[8,2048]{1,0:T(8,128)S(1)}) custom-call(bf16[128,2048]{1,0:T(8,128)(2,1)S(1)} %get-tuple-element.23.q_ref, bf16[128,2048]{1,0:T(8,128)(2,1)S(1)} %get-tuple-element.24.g_ref, bf16[256,256]{1,0:T(8,128)(2,1)S(1)} %collective-permute-done.1.v_ref, ...), custom_call_target="tpu_custom_call" | custom-call | flops 268435456 | bytes 3538944 | tf_op jit(solution)/shard_map/pallas_call | solution.py:250
  11.3 1.8 %collective-permute-start.2 = (bf16[256,256]{1,0:T(8,128)(2,1)S(1)}, bf16[256,256]{1,0:T(8,128)(2,1)S(1)}, u32[]{:S(2)}, u32[]{:S(2)}) collective-permute-start(bf16[256,256]{1,0:T(8,128)(2,1)S(1)} %bitcast.4), channel_id=1, source_target_pairs={{0,16},{16,0},{1,17},{17,1},{2,18},{18,2},{3,19},{19,3},{4,20},{20... | collective-permute-start | bytes 393224 | tf_op jit(solution)/shard_map/ppermute | solution.py:276
  13.1 0.3 %collective-permute-start.3 = (bf16[256,256]{1,0:T(8,128)(2,1)S(1)}, bf16[256,256]{1,0:T(8,128)(2,1)S(1)}, u32[]{:S(2)}, u32[]{:S(2)}) collective-permute-start(bf16[256,256]{1,0:T(8,128)(2,1)S(1)} %bitcast.3), channel_id=1, source_target_pairs={{0,16},{16,0},{1,17},{17,1},{2,18},{18,2},{3,19},{19,3},{4,20},{20... | collective-permute-start | bytes 393224 | tf_op jit(solution)/shard_map/ppermute | solution.py:276
  13.4 2.3 %shard_map.149 = (bf16[128,2048]{1,0:T(8,128)(2,1)}, bf16[128,256]{1,0:T(8,128)(2,1)}, bf16[128,256]{1,0:T(8,128)(2,1)}, f32[256,256]{1,0:T(8,128)S(1)}, f32[256,256]{1,0:T(8,128)S(1)}) custom-call(bf16[128,2048]{1,0:T(8,128)(2,1)S(1)} %get-tuple-element.23.q_ref, bf16[128,2048]{1,0:T(8,128)(2,1)S(1)} %get-tuple-element.24.g_ref, ...), custom_call_target="tpu_custom_call" | custom-call | flops 738197504 | bytes 10027008 | tf_op jit(solution)/shard_map/pallas_call | solution.py:250
  15.7 1.8 %collective-permute-done.2 = bf16[256,256]{1,0:T(8,128)(2,1)S(1)} collective-permute-done((bf16[256,256]{1,0:T(8,128)(2,1)S(1)}, bf16[256,256]{1,0:T(8,128)(2,1)S(1)}, u32[]{:S(2)}, u32[]{:S(2)}) %collective-permute-start.2) | collective-permute-done | bytes 131104 | tf_op jit(solution)/shard_map/ppermute | solution.py:276
  17.4 0.7 %convert_add_fusion.1 = f32[256,256]{1,0:T(8,128)} fusion(f32[256,256]{1,0:T(8,128)S(1)} %get-tuple-element.37, bf16[256,256]{1,0:T(8,128)(2,1)S(1)} %collective-permute-done.2), kind=kLoop, calls=%fused_computation.1 | loop fusion | flops 131072 | bytes 655360 | tf_op jit(solution)/shard_map/add | solution.py:359
  18.2 0.7 %collective-permute-done.3 = bf16[256,256]{1,0:T(8,128)(2,1)S(1)} collective-permute-done((bf16[256,256]{1,0:T(8,128)(2,1)S(1)}, bf16[256,256]{1,0:T(8,128)(2,1)S(1)}, u32[]{:S(2)}, u32[]{:S(2)}) %collective-permute-start.3) | collective-permute-done | bytes 131104 | tf_op jit(solution)/shard_map/ppermute | solution.py:276
  18.8 0.7 %convert_add_fusion = f32[256,256]{1,0:T(8,128)} fusion(f32[256,256]{1,0:T(8,128)S(1)} %get-tuple-element.39, bf16[256,256]{1,0:T(8,128)(2,1)S(1)} %collective-permute-done.3), kind=kLoop, calls=%fused_computation | loop fusion | flops 131072 | bytes 655360 | tf_op jit(solution)/shard_map/add | solution.py:360
Async XLA Ops:
  0.6 7.5 %collective-permute-start = (bf16[256,256]{1,0:T(8,128)(2,1)}, bf16[256,256]{1,0:T(8,128)(2,1)S(1)}, u32[]{:S(2)}, u32[]{:S(2)}) collective-permute-start(bf16[256,256]{1,0:T(8,128)(2,1)} %ok_in.1), channel_id=1, source_target_pairs={{0,16},{16,0},{1,17},{17,1},{2,18},{18,2},{3,19},{19,3},{4,20},{20... | collective-permute-start | bytes 393224 | tf_op jit(solution)/shard_map/ppermute | solution.py:276
  3.6 6.5 %collective-permute-start.1 = (bf16[256,256]{1,0:T(8,128)(2,1)}, bf16[256,256]{1,0:T(8,128)(2,1)S(1)}, u32[]{:S(2)}, u32[]{:S(2)}) collective-permute-start(bf16[256,256]{1,0:T(8,128)(2,1)} %ov_in.1), channel_id=1, source_target_pairs={{0,16},{16,0},{1,17},{17,1},{2,18},{18,2},{3,19},{19,3},{4,20},{20... | collective-permute-start | bytes 393224 | tf_op jit(solution)/shard_map/ppermute | solution.py:276
  11.3 6.2 %collective-permute-start.2 = (bf16[256,256]{1,0:T(8,128)(2,1)S(1)}, bf16[256,256]{1,0:T(8,128)(2,1)S(1)}, u32[]{:S(2)}, u32[]{:S(2)}) collective-permute-start(bf16[256,256]{1,0:T(8,128)(2,1)S(1)} %bitcast.4), channel_id=1, source_target_pairs={{0,16},{16,0},{1,17},{17,1},{2,18},{18,2},{3,19},{19,3},{4,20},{20... | collective-permute-start | bytes 393224 | tf_op jit(solution)/shard_map/ppermute | solution.py:276
  13.1 5.8 %collective-permute-start.3 = (bf16[256,256]{1,0:T(8,128)(2,1)S(1)}, bf16[256,256]{1,0:T(8,128)(2,1)S(1)}, u32[]{:S(2)}, u32[]{:S(2)}) collective-permute-start(bf16[256,256]{1,0:T(8,128)(2,1)S(1)} %bitcast.3), channel_id=1, source_target_pairs={{0,16},{16,0},{1,17},{17,1},{2,18},{18,2},{3,19},{19,3},{4,20},{20... | collective-permute-start | bytes 393224 | tf_op jit(solution)/shard_map/ppermute | solution.py:276

commit v3 on v2

--- a/solution.py
+++ b/solution.py
@@ -210,6 +210,13 @@
             back_ref[shift, :, cols] = dk[shift * own_keys : (shift + 1) * own_keys]
 
 
+def sum_kernel(after_ref, own_ref, *refs):
+    total = own_ref[...]
+    for ref in refs[:-1]:
+        total = total + ref[...].astype(F32)
+    refs[-1][...] = total
+
+
 def last_kernel(
     unroll, q_ref, g_ref, k_ref, p_ref, d_ref, fin_ref, delta_ref, fk_ref, fds_ref,
     dq_ref, dtk_ref, dtv_ref, dok_ref, dov_ref, low_ref, ds_ref,
@@ -355,9 +362,20 @@
         mib,
         q, g, near_k, near_p, near_d, fin, delta, far_k, far_ds,
     )
-    for key_block, value_block in zip(returned_k, returned_v):
-        dok = dok + key_block.astype(F32)
-        dov = dov + value_block.astype(F32)
+
+    def summed(after, own_sum, returned):
+        return call(
+            sum_kernel,
+            [pltpu.HBM] + [pltpu.VMEM] * (1 + len(returned)),
+            [shape(own_sum.shape, F32)],
+            [],
+            0,
+            mib,
+            pltpu.with_memory_space_constraint(after, pltpu.HBM), own_sum, *returned,
+        )[0]
+
+    dov = summed(dq, dov, returned_v)
+    dok = summed(dov, dok, returned_k)
     return dq, dtk, dtv, dok, dov
 
 

time: 19.7 us -> 18.5 us (0.939)
  waiting for transfers between devices: 4.22 us -> 2.46 us
  Pallas kernels: 7.42 us -> 8.88 us
  other arithmetic: 1.45 us -> 0 us
  starting transfers between devices: 5.17 us -> 5.7 us
    ppermute x4, waiting for transfers between devices: 4.22 us -> 2.46 us  [shifted(): return lax.ppermute(x, 'ctx', [(o, (o - shift) % ctx) for o in range(ctx)])]
    pallas_call x4 -> x6, Pallas kernels: 7.42 us -> 8.88 us  [call(): pl.pallas_call(kernel, out_shape=outs, in_specs=[pl.BlockSpec(memory_spac...]
    add x2 -> x0, other arithmetic: 1.45 us -> none  [the longest x1 0.73 us: body(): dok = dok + key_block.astype(F32)]
    ppermute x4, starting transfers between devices: 5.17 us -> 5.7 us  [shifted(): return lax.ppermute(x, 'ctx', [(o, (o - shift) % ctx) for o in range(ctx)])]
  transfers between devices with their start and end apart: 4 -> 4, of which waited for: 4 -> 3; matrix products, arithmetic and copies ran while one was open for 4% -> 0% of each run, Pallas kernels for 32% -> 44%
where the time goes in v3:
time: 18.5 us; the launch traced here: 18.4 us
  Pallas kernels  8.88 us (48%)
  starting transfers between devices  5.7 us (31%)
  waiting for transfers between devices  2.46 us (13%)
  between operations  1.31 us (7%)
    pallas_call x6, Pallas kernels, call(): pl.pallas_call(kernel, out_shape=outs, in_specs=[pl.BlockSpec(memory_spac...  8.88 us
    ppermute x4, starting transfers between devices, shifted(): return lax.ppermute(x, 'ctx', [(o, (o - shift) % ctx) for o in range(ctx)])  5.7 us
    ppermute x4, waiting for transfers between devices, shifted(): return lax.ppermute(x, 'ctx', [(o, (o - shift) % ctx) for o in range(ctx)])  2.46 us
  transfers between devices with their start and end apart: 4, of which 3 were waited for; matrix products, arithmetic and copies ran while one was open for 0% of the time, Pallas kernels for 44%

profile of v3, /device:TPU:0, one launch (start us, length us, event | category | flops | bytes accessed | tf_op | source)
XLA Modules:
  0.0 18.4 jit_solution(8253152289412474526)
XLA Ops:
  0.6 3.0 %collective-permute-start = (bf16[256,256]{1,0:T(8,128)(2,1)}, bf16[256,256]{1,0:T(8,128)(2,1)S(1)}, u32[]{:S(2)}, u32[]{:S(2)}) collective-permute-start(bf16[256,256]{1,0:T(8,128)(2,1)} %ok_in.1), channel_id=1, source_target_pairs={{0,16},{16,0},{1,17},{17,1},{2,18},{18,2},{3,19},{19,3},{4,20},{20... | collective-permute-start | bytes 393224 | tf_op jit(solution)/shard_map/ppermute | solution.py:283
  3.6 0.1 collective-permute-start.1
  4.4 2.9 %shard_map.146 = (bf16[128,2048]{1,0:T(8,128)(2,1)S(1)}, bf16[128,2048]{1,0:T(8,128)(2,1)S(1)}, bf16[384,256]{1,0:T(8,128)(2,1)S(1)}, f32[2,384,1024]{2,1,0:T(8,...) custom-call(bf16[128,2048]{1,0:T(8,128)(2,1)} %q_in.1, ...), custom_call_target="tpu_custom_call" | custom-call | flops 402653184 | bytes 9048868 | tf_op jit(solution)/shard_map/pallas_call | solution.py:257
  7.2 0.9 %collective-permute-done.k_ref.fk_ref = bf16[256,256]{1,0:T(8,128)(2,1)S(1)} collective-permute-done((bf16[256,256]{1,0:T(8,128)(2,1)}, bf16[256,256]{1,0:T(8,128)(2,1)S(1)}, u32[]{:S(2)}, u32[]{:S(2)}) %collective-permute-start) | collective-permute-done | bytes 131104 | tf_op jit(solution)/shard_map/ppermute | solution.py:283
  8.2 1.2 %shard_map.147 = (bf16[1,256,256]{2,1,0:T(8,128)(2,1)S(1)}, bf16[2,256,1024]{2,1,0:T(8,128)(2,1)S(1)}, f32[8,2048]{1,0:T(8,128)S(1)}) custom-call(bf16[128,2048]{1,0:T(8,128)(2,1)S(1)} %get-tuple-element.23.q_ref, bf16[128,2048]{1,0:T(8,128)(2,1)S(1)} %get-tuple-element.24.g_ref, bf16[256,256]{1,0:T(8,128)(2,1)S(1)} %collective-permute-done.k_ref.fk_ref, ...), custom_call_target="tpu_custom_call" | custom-call | flops 268435456 | bytes 2494464 | tf_op jit(solution)/shard_map/pallas_call | solution.py:257
  9.3 2.1 %collective-permute-start.2 = (bf16[256,256]{1,0:T(8,128)(2,1)S(1)}, bf16[256,256]{1,0:T(8,128)(2,1)S(1)}, u32[]{:S(2)}, u32[]{:S(2)}) collective-permute-start(bf16[256,256]{1,0:T(8,128)(2,1)S(1)} %bitcast.3), channel_id=1, source_target_pairs={{0,16},{16,0},{1,17},{17,1},{2,18},{18,2},{3,19},{19,3},{4,20},{20... | collective-permute-start | bytes 393224 | tf_op jit(solution)/shard_map/ppermute | solution.py:283
  11.5 0.0 collective-permute-done.1.v_ref
  11.5 1.1 %shard_map.148 = (bf16[1,256,256]{2,1,0:T(8,128)(2,1)S(1)}, bf16[2,256,1024]{2,1,0:T(8,128)(2,1)S(1)}, f32[8,2048]{1,0:T(8,128)S(1)}) custom-call(bf16[128,2048]{1,0:T(8,128)(2,1)S(1)} %get-tuple-element.23.q_ref, bf16[128,2048]{1,0:T(8,128)(2,1)S(1)} %get-tuple-element.24.g_ref, bf16[256,256]{1,0:T(8,128)(2,1)S(1)} %collective-permute-done.1.v_ref, ...), custom_call_target="tpu_custom_call" | custom-call | flops 268435456 | bytes 3538944 | tf_op jit(solution)/shard_map/pallas_call | solution.py:257
  12.6 0.5 %collective-permute-start.3 = (bf16[256,256]{1,0:T(8,128)(2,1)S(1)}, bf16[256,256]{1,0:T(8,128)(2,1)S(1)}, u32[]{:S(2)}, u32[]{:S(2)}) collective-permute-start(bf16[256,256]{1,0:T(8,128)(2,1)S(1)} %bitcast.4), channel_id=1, source_target_pairs={{0,16},{16,0},{1,17},{17,1},{2,18},{18,2},{3,19},{19,3},{4,20},{20... | collective-permute-start | bytes 393224 | tf_op jit(solution)/shard_map/ppermute | solution.py:283
  13.1 2.3 %shard_map.149 = (bf16[128,2048]{1,0:T(8,128)(2,1)}, bf16[128,256]{1,0:T(8,128)(2,1)}, bf16[128,256]{1,0:T(8,128)(2,1)}, f32[256,256]{1,0:T(8,128)S(1)}, f32[256,256]{1,0:T(8,128)S(1)}) custom-call(bf16[128,2048]{1,0:T(8,128)(2,1)S(1)} %get-tuple-element.23.q_ref, bf16[128,2048]{1,0:T(8,128)(2,1)S(1)} %get-tuple-element.24.g_ref, ...), custom_call_target="tpu_custom_call" | custom-call | flops 738197504 | bytes 10027008 | tf_op jit(solution)/shard_map/pallas_call | solution.py:257
  15.4 0.2 %collective-permute-done.2.refs_0_ = bf16[256,256]{1,0:T(8,128)(2,1)S(1)} collective-permute-done((bf16[256,256]{1,0:T(8,128)(2,1)S(1)}, bf16[256,256]{1,0:T(8,128)(2,1)S(1)}, u32[]{:S(2)}, u32[]{:S(2)}) %collective-permute-start.2) | collective-permute-done | bytes 131104 | tf_op jit(solution)/shard_map/ppermute | solution.py:283
  15.6 0.7 %shard_map.150.after_ref = f32[256,256]{1,0:T(8,128)} custom-call(bf16[128,2048]{1,0:T(8,128)(2,1)} %get-tuple-element.18.after_ref, f32[256,256]{1,0:T(8,128)S(1)} %get-tuple-element.37.own_ref, bf16[256,256]{1,0:T(8,128)(2,1)S(1)} %collective-permute-done.2.refs_0_), custom_call_target="tpu_custom_call" | custom-call | bytes 1179648 | tf_op jit(solution)/shard_map/pallas_call | solution.py:257
  16.3 1.3 %collective-permute-done.3.refs_0_ = bf16[256,256]{1,0:T(8,128)(2,1)S(1)} collective-permute-done((bf16[256,256]{1,0:T(8,128)(2,1)S(1)}, bf16[256,256]{1,0:T(8,128)(2,1)S(1)}, u32[]{:S(2)}, u32[]{:S(2)}) %collective-permute-start.3) | collective-permute-done | bytes 131104 | tf_op jit(solution)/shard_map/ppermute | solution.py:283
  17.6 0.7 %shard_map.151 = f32[256,256]{1,0:T(8,128)} custom-call(f32[256,256]{1,0:T(8,128)} %shard_map.150.after_ref, f32[256,256]{1,0:T(8,128)S(1)} %get-tuple-element.39.own_ref, bf16[256,256]{1,0:T(8,128)(2,1)S(1)} %collective-permute-done.3.refs_0_), custom_call_target="tpu_custom_call" | custom-call | bytes 917504 | tf_op jit(solution)/shard_map/pallas_call | solution.py:257
Async XLA Ops:
  0.6 7.5 %collective-permute-start = (bf16[256,256]{1,0:T(8,128)(2,1)}, bf16[256,256]{1,0:T(8,128)(2,1)S(1)}, u32[]{:S(2)}, u32[]{:S(2)}) collective-permute-start(bf16[256,256]{1,0:T(8,128)(2,1)} %ok_in.1), channel_id=1, source_target_pairs={{0,16},{16,0},{1,17},{17,1},{2,18},{18,2},{3,19},{19,3},{4,20},{20... | collective-permute-start | bytes 393224 | tf_op jit(solution)/shard_map/ppermute | solution.py:283
  3.6 7.8 %collective-permute-start.1 = (bf16[256,256]{1,0:T(8,128)(2,1)}, bf16[256,256]{1,0:T(8,128)(2,1)S(1)}, u32[]{:S(2)}, u32[]{:S(2)}) collective-permute-start(bf16[256,256]{1,0:T(8,128)(2,1)} %ov_in.1), channel_id=1, source_target_pairs={{0,16},{16,0},{1,17},{17,1},{2,18},{18,2},{3,19},{19,3},{4,20},{20... | collective-permute-start | bytes 393224 | tf_op jit(solution)/shard_map/ppermute | solution.py:283
  9.3 6.3 %collective-permute-start.2 = (bf16[256,256]{1,0:T(8,128)(2,1)S(1)}, bf16[256,256]{1,0:T(8,128)(2,1)S(1)}, u32[]{:S(2)}, u32[]{:S(2)}) collective-permute-start(bf16[256,256]{1,0:T(8,128)(2,1)S(1)} %bitcast.3), channel_id=1, source_target_pairs={{0,16},{16,0},{1,17},{17,1},{2,18},{18,2},{3,19},{19,3},{4,20},{20... | collective-permute-start | bytes 393224 | tf_op jit(solution)/shard_map/ppermute | solution.py:283
  12.6 5.0 %collective-permute-start.3 = (bf16[256,256]{1,0:T(8,128)(2,1)S(1)}, bf16[256,256]{1,0:T(8,128)(2,1)S(1)}, u32[]{:S(2)}, u32[]{:S(2)}) collective-permute-start(bf16[256,256]{1,0:T(8,128)(2,1)S(1)} %bitcast.4), channel_id=1, source_target_pairs={{0,16},{16,0},{1,17},{17,1},{2,18},{18,2},{3,19},{19,3},{4,20},{20... | collective-permute-start | bytes 393224 | tf_op jit(solution)/shard_map/ppermute | solution.py:283

commit v4 on v3

--- a/solution.py
+++ b/solution.py
@@ -11,6 +11,7 @@
 WIDTH = 128
 TILE = 128
 PAIR = 2 * WIDTH
+NEAR_OUTS = 7
 NEG = -1e30
 SCALE = 1.0 / math.sqrt(WIDTH)
 SCALE2 = SCALE * math.log2(math.e)
@@ -98,7 +99,15 @@
     return twice(jnp.where(allowed, 0.0, NEG).astype(F32))
 
 
-def near_kernel(
+def near_kernel(ctx, odd, *refs):
+    ins, rest = refs[:11], refs[11 if odd else 11 + NEAR_OUTS :]
+
+    @pl.when(lax.rem(lax.axis_index("dp"), 2) == int(odd))
+    def work():
+        near_work(ctx, *ins, *rest)
+
+
+def near_work(
     ctx, q_in, g_in, tk_in, tv_in, ok_in, ov_in, rl_in, ro_in, rt_in, rs_in, rc_ref,
     q_ref, g_ref, k_ref, p_ref, d_ref, stats_ref, table_ref,
     v_ref, rl_ref, ro_ref, rt_ref, rs_ref, sems,
@@ -249,7 +258,7 @@
         dov_ref[:, cols] = dv[tail:]
 
 
-def call(kernel, spaces, outs, scratch, flops, mib, *args):
+def call(kernel, spaces, outs, scratch, flops, mib, *args, aliases={}):
     vmem = pl.BlockSpec(memory_space=pltpu.VMEM)
     moved = sum(a.size * a.dtype.itemsize for a in args) + sum(
         math.prod(o.shape) * o.dtype.itemsize for o in outs
@@ -260,6 +269,7 @@
         in_specs=[pl.BlockSpec(memory_space=space) for space in spaces],
         out_specs=[vmem] * len(outs),
         scratch_shapes=scratch,
+        input_output_aliases=aliases,
         compiler_params=pltpu.CompilerParams(vmem_limit_bytes=mib * 2**20),
         cost_estimate=pl.CostEstimate(flops=flops, bytes_accessed=moved, transcendentals=0),
     )(*args)
@@ -283,7 +293,6 @@
         return lax.ppermute(x, "ctx", [(o, (o - shift) % ctx) for o in range(ctx)])
 
     far_k = [shifted(ck, s) for s in range(1, ctx)]
-    far_v = [shifted(cv, s) for s in range(1, ctx)]
     shape = jax.ShapeDtypeStruct
     product = 2 * q_width * rows * WIDTH
     small = read_owner.shape
@@ -291,18 +300,18 @@
         pltpu.with_memory_space_constraint(a, pltpu.HBM)
         for a in (q, g, tk, tv, ck, cv, row_list, read_owner, read_tile, read_list)
     ]
-    q, g, near_k, near_p, near_d, stats, table = call(
-        functools.partial(near_kernel, ctx),
+    near_outs = [
+        shape(q.shape, BF16),
+        shape(g.shape, BF16),
+        shape((near_keys, kv_width), BF16),
+        shape((heads, near_keys, group_rows), F32),
+        shape((heads, near_keys, group_rows), F32),
+        shape((8, heads * group_rows), F32),
+        shape((slots, rows), F32),
+    ]
+    near = [
         [pltpu.HBM] * len(here) + [pltpu.SMEM],
-        [
-            shape(q.shape, BF16),
-            shape(g.shape, BF16),
-            shape((near_keys, kv_width), BF16),
-            shape((heads, near_keys, group_rows), F32),
-            shape((heads, near_keys, group_rows), F32),
-            shape((8, heads * group_rows), F32),
-            shape((slots, rows), F32),
-        ],
+        near_outs,
         [
             pltpu.VMEM((near_keys, kv_width), BF16),
             pltpu.VMEM(row_list.shape, jnp.int32),
@@ -314,6 +323,15 @@
         2 * product * near_keys // WIDTH,
         32,
         *here, read_count,
+    ]
+    early = list(call(functools.partial(near_kernel, ctx, True), *near))
+    own_v, early[-1] = lax.optimization_barrier((cv, early[-1]))
+    far_v = [shifted(own_v, s) for s in range(1, ctx)]
+    near[0] = near[0] + [pltpu.VMEM] * NEAR_OUTS
+    first = len(here) + 1
+    q, g, near_k, near_p, near_d, stats, table = call(
+        functools.partial(near_kernel, ctx, False), *near, *early,
+        aliases={first + i: i for i in range(NEAR_OUTS)},
     )
     mib = 32 if unroll else 60
     total = [] if unroll else [pltpu.VMEM((far_keys, WIDTH), F32)]

time: 18.5 us -> 18.3 us (0.989)
  waiting for transfers between devices: 2.46 us -> 2.25 us
    ppermute x4, waiting for transfers between devices: 2.46 us -> 2.25 us  [shifted(): return lax.ppermute(x, 'ctx', [(o, (o - shift) % ctx) for o in range(ctx)])]
    pallas_call x6 -> x7, Pallas kernels: 8.88 us -> 9.02 us  [call(): pl.pallas_call(kernel, out_shape=outs, in_specs=[pl.BlockSpec(memory_spac...]
  transfers between devices with their start and end apart: 4 -> 4, of which waited for: 3 -> 1; matrix products, arithmetic and copies ran while one was open for 0% -> 0% of each run, Pallas kernels for 44% -> 46%
where the time goes in v4:
time: 18.3 us; the launch traced here: 18.2 us
  Pallas kernels  9.02 us (49%)
  starting transfers between devices  5.6 us (31%)
  waiting for transfers between devices  2.25 us (12%)
  between operations  1.33 us (7%)
    pallas_call x7, Pallas kernels, call(): pl.pallas_call(kernel, out_shape=outs, in_specs=[pl.BlockSpec(memory_spac...  9.02 us
    ppermute x4, starting transfers between devices, shifted(): return lax.ppermute(x, 'ctx', [(o, (o - shift) % ctx) for o in range(ctx)])  5.6 us
    ppermute x4, waiting for transfers between devices, shifted(): return lax.ppermute(x, 'ctx', [(o, (o - shift) % ctx) for o in range(ctx)])  2.25 us
  transfers between devices with their start and end apart: 4, of which 1 were waited for; matrix products, arithmetic and copies ran while one was open for 0% of the time, Pallas kernels for 46%

profile of v4, /device:TPU:0, one launch (start us, length us, event | category | flops | bytes accessed | tf_op | source)
XLA Modules:
  0.0 18.2 jit_solution(2672341863762038303)
XLA Ops:
  0.6 3.0 %collective-permute-start = (bf16[256,256]{1,0:T(8,128)(2,1)}, bf16[256,256]{1,0:T(8,128)(2,1)S(1)}, u32[]{:S(2)}, u32[]{:S(2)}) collective-permute-start(bf16[256,256]{1,0:T(8,128)(2,1)} %refs_4_.3), channel_id=1, source_target_pairs={{0,16},{16,0},{1,17},{17,1},{2,18},{18,2},{3,19},{19,3},{4,20},{20... | collective-permute-start | bytes 393224 | tf_op jit(solution)/shard_map/ppermute | solution.py:293
  4.3 0.1 shard_map.146
  4.4 0.1 collective-permute-start.1
  4.5 2.9 %shard_map.147 = (bf16[128,2048]{1,0:T(8,128)(2,1)S(1)}, bf16[128,2048]{1,0:T(8,128)(2,1)S(1)}, bf16[384,256]{1,0:T(8,128)(2,1)S(1)}, f32[2,384,1024]{2,1,0:T(8,...) custom-call(bf16[128,2048]{1,0:T(8,128)(2,1)} %refs_0_.3, ...), custom_call_target="tpu_custom_call", output_to_operand_aliasing={{0}: (11, {}), {1}: (12, {}), {2}: (13, {}), {3}: (14, {}),... | custom-call | flops 402653184 | bytes 16655140 | tf_op jit(solution)/shard_map/pallas_call | solution.py:266
  7.4 0.0 collective-permute-done.k_ref.fk_ref
  7.4 1.2 %shard_map.148 = (bf16[1,256,256]{2,1,0:T(8,128)(2,1)S(1)}, bf16[2,256,1024]{2,1,0:T(8,128)(2,1)S(1)}, f32[8,2048]{1,0:T(8,128)S(1)}) custom-call(bf16[128,2048]{1,0:T(8,128)(2,1)S(1)} %get-tuple-element.40.q_ref, bf16[128,2048]{1,0:T(8,128)(2,1)S(1)} %get-tuple-element.41.g_ref, bf16[256,256]{1,0:T(8,128)(2,1)S(1)} %collective-permute-done.k_ref.fk_ref, ...), custom_call_target="tpu_custom_call" | custom-call | flops 268435456 | bytes 2494464 | tf_op jit(solution)/shard_map/pallas_call | solution.py:266
  8.6 2.1 %collective-permute-start.2 = (bf16[256,256]{1,0:T(8,128)(2,1)S(1)}, bf16[256,256]{1,0:T(8,128)(2,1)S(1)}, u32[]{:S(2)}, u32[]{:S(2)}) collective-permute-start(bf16[256,256]{1,0:T(8,128)(2,1)S(1)} %bitcast.3), channel_id=1, source_target_pairs={{0,16},{16,0},{1,17},{17,1},{2,18},{18,2},{3,19},{19,3},{4,20},{20... | collective-permute-start | bytes 393224 | tf_op jit(solution)/shard_map/ppermute | solution.py:293
  10.6 0.0 collective-permute-done.1.v_ref
  10.6 1.1 %shard_map.149 = (bf16[1,256,256]{2,1,0:T(8,128)(2,1)S(1)}, bf16[2,256,1024]{2,1,0:T(8,128)(2,1)S(1)}, f32[8,2048]{1,0:T(8,128)S(1)}) custom-call(bf16[128,2048]{1,0:T(8,128)(2,1)S(1)} %get-tuple-element.40.q_ref, bf16[128,2048]{1,0:T(8,128)(2,1)S(1)} %get-tuple-element.41.g_ref, bf16[256,256]{1,0:T(8,128)(2,1)S(1)} %collective-permute-done.1.v_ref, ...), custom_call_target="tpu_custom_call" | custom-call | flops 268435456 | bytes 3538944 | tf_op jit(solution)/shard_map/pallas_call | solution.py:266
  11.7 0.5 %collective-permute-start.3 = (bf16[256,256]{1,0:T(8,128)(2,1)S(1)}, bf16[256,256]{1,0:T(8,128)(2,1)S(1)}, u32[]{:S(2)}, u32[]{:S(2)}) collective-permute-start(bf16[256,256]{1,0:T(8,128)(2,1)S(1)} %bitcast.4), channel_id=1, source_target_pairs={{0,16},{16,0},{1,17},{17,1},{2,18},{18,2},{3,19},{19,3},{4,20},{20... | collective-permute-start | bytes 393224 | tf_op jit(solution)/shard_map/ppermute | solution.py:293
  12.2 2.3 %shard_map.150 = (bf16[128,2048]{1,0:T(8,128)(2,1)}, bf16[128,256]{1,0:T(8,128)(2,1)}, bf16[128,256]{1,0:T(8,128)(2,1)}, f32[256,256]{1,0:T(8,128)S(1)}, f32[256,256]{1,0:T(8,128)S(1)}) custom-call(bf16[128,2048]{1,0:T(8,128)(2,1)S(1)} %get-tuple-element.40.q_ref, bf16[128,2048]{1,0:T(8,128)(2,1)S(1)} %get-tuple-element.41.g_ref, ...), custom_call_target="tpu_custom_call" | custom-call | flops 738197504 | bytes 10027008 | tf_op jit(solution)/shard_map/pallas_call | solution.py:266
  14.5 0.0 collective-permute-done.2.refs_0_
  14.5 0.7 %shard_map.151.after_ref = f32[256,256]{1,0:T(8,128)} custom-call(bf16[128,2048]{1,0:T(8,128)(2,1)} %get-tuple-element.27.after_ref, f32[256,256]{1,0:T(8,128)S(1)} %get-tuple-element.55.own_ref, bf16[256,256]{1,0:T(8,128)(2,1)S(1)} %collective-permute-done.2.refs_0_), custom_call_target="tpu_custom_call" | custom-call | bytes 1179648 | tf_op jit(solution)/shard_map/pallas_call | solution.py:266
  15.2 2.2 %collective-permute-done.3.refs_0_ = bf16[256,256]{1,0:T(8,128)(2,1)S(1)} collective-permute-done((bf16[256,256]{1,0:T(8,128)(2,1)S(1)}, bf16[256,256]{1,0:T(8,128)(2,1)S(1)}, u32[]{:S(2)}, u32[]{:S(2)}) %collective-permute-start.3) | collective-permute-done | bytes 131104 | tf_op jit(solution)/shard_map/ppermute | solution.py:293
  17.5 0.7 %shard_map.152 = f32[256,256]{1,0:T(8,128)} custom-call(f32[256,256]{1,0:T(8,128)} %shard_map.151.after_ref, f32[256,256]{1,0:T(8,128)S(1)} %get-tuple-element.57.own_ref, bf16[256,256]{1,0:T(8,128)(2,1)S(1)} %collective-permute-done.3.refs_0_), custom_call_target="tpu_custom_call" | custom-call | bytes 917504 | tf_op jit(solution)/shard_map/pallas_call | solution.py:266
Async XLA Ops:
  0.6 6.8 %collective-permute-start = (bf16[256,256]{1,0:T(8,128)(2,1)}, bf16[256,256]{1,0:T(8,128)(2,1)S(1)}, u32[]{:S(2)}, u32[]{:S(2)}) collective-permute-start(bf16[256,256]{1,0:T(8,128)(2,1)} %refs_4_.3), channel_id=1, source_target_pairs={{0,16},{16,0},{1,17},{17,1},{2,18},{18,2},{3,19},{19,3},{4,20},{20... | collective-permute-start | bytes 393224 | tf_op jit(solution)/shard_map/ppermute | solution.py:293
  4.4 6.2 %collective-permute-start.1 = (bf16[256,256]{1,0:T(8,128)(2,1)}, bf16[256,256]{1,0:T(8,128)(2,1)S(1)}, u32[]{:S(2)}, u32[]{:S(2)}) collective-permute-start(bf16[256,256]{1,0:T(8,128)(2,1)} %refs_5_.3), channel_id=1, source_target_pairs={{0,16},{16,0},{1,17},{17,1},{2,18},{18,2},{3,19},{19,3},{4,20},{20... | collective-permute-start | bytes 393224 | tf_op jit(solution)/shard_map/ppermute | solution.py:293
  8.6 5.9 %collective-permute-start.2 = (bf16[256,256]{1,0:T(8,128)(2,1)S(1)}, bf16[256,256]{1,0:T(8,128)(2,1)S(1)}, u32[]{:S(2)}, u32[]{:S(2)}) collective-permute-start(bf16[256,256]{1,0:T(8,128)(2,1)S(1)} %bitcast.3), channel_id=1, source_target_pairs={{0,16},{16,0},{1,17},{17,1},{2,18},{18,2},{3,19},{19,3},{4,20},{20... | collective-permute-start | bytes 393224 | tf_op jit(solution)/shard_map/ppermute | solution.py:293
  11.7 5.7 %collective-permute-start.3 = (bf16[256,256]{1,0:T(8,128)(2,1)S(1)}, bf16[256,256]{1,0:T(8,128)(2,1)S(1)}, u32[]{:S(2)}, u32[]{:S(2)}) collective-permute-start(bf16[256,256]{1,0:T(8,128)(2,1)S(1)} %bitcast.4), channel_id=1, source_target_pairs={{0,16},{16,0},{1,17},{17,1},{2,18},{18,2},{3,19},{19,3},{4,20},{20... | collective-permute-start | bytes 393224 | tf_op jit(solution)/shard_map/ppermute | solution.py:293
